TPU v7x, 32 devices: a whole 2x2x4 slice. The times are simulated.
32 devices in a mesh: groups: 2 (over y), lat: 4 (over z), lon: 2 (over x), lev: 2 (over core).
Axes of the slice: x: 2, y: 2, z: 4, core: 2. Of those that a mesh axis runs over, the one named last changes fastest.
Arguments:
- model_field: bfloat16 [16, 128, 4, 2, 1024], P('groups', 'lev', 'lat', 'lon'), parts along dimension 0, may hold values from -6 to 6
- interp_weights: bfloat16 [4, 2, 8, 2, 128, 128], P('lat', 'lon'), may hold values from -0.375 to 0.375
- interp_blocks: int32 [4, 2, 8, 2], P('lat', 'lon'), may hold values from 0 to 7
- send_list: int32 [4, 2, 2], P('lat', 'lon'), may hold values from 0 to 7
- send_count: int32 [4, 2], P('lat', 'lon'), may hold values from 1 to 2
- conv_weights: bfloat16 [4, 2, 8, 10, 128, 128], P('lat', 'lon'), may hold values from -0.15625 to 0.15625
- neighbours: int32 [4, 2, 8, 10], P('lat', 'lon'), may hold values from 0 to 37
Outputs:
- subgrid_field: bfloat16 [16, 128, 4, 2, 1024], P('groups', 'lev', 'lat', 'lon'), parts along dimension 0
There are 2 independent parts, one for each index of `groups`. A program takes and returns all parts, laid end to end along the dimension named above; an argument that names none is the same for every part. Nothing has to cross between parts.
All inputs are finite; a program needn't handle non-finite values.
Results may differ from a plain program's by a relative error of at most 0.0049.
Values may be sent and summed in bfloat16 or wider, within the bound.
A program may use at most 64 MiB of HBM per device.

v0:
```python
import jax
import jax.numpy as jnp
from jax import lax
from jax.sharding import PartitionSpec as P


def from_behind(block, axis, distance):
    devices = range(lax.axis_size(axis))
    route = [((i - distance) % len(devices), i) for i in devices]
    return lax.ppermute(block, axis, route)


def from_behind_2(shard, axis, by):
    peers = lax.axis_size(axis)
    pairs = [(i, i + by) for i in range(peers) if 0 <= i + by < peers]
    return lax.ppermute(shard, axis, pairs)


def body(
    model_field, interp_weights, interp_blocks, send_list, send_count, conv_weights, neighbours
):
    members = model_field.shape[0]
    levels = model_field.shape[1]
    width = interp_weights.shape[-1]
    rows = members * levels
    cells = model_field.reshape(rows, -1, width)
    picked = cells[:, interp_blocks[0, 0], :]
    sub = jnp.einsum(
        "rkqc,kqcd->rkd", picked, interp_weights[0, 0], preferred_element_type=jnp.float32
    ).astype(jnp.bfloat16)
    slots = send_list[0, 0]
    live = jnp.arange(slots.shape[0], dtype=jnp.int32) < send_count[0, 0]
    packed = jnp.where(live[None, :, None], sub[:, slots, :], jnp.zeros((), jnp.bfloat16))
    lon_parts = [packed]
    for step in (1, -1):
        lon_parts.append(from_behind(packed, "lon", step))
    stacked = jnp.stack(lon_parts, 1)
    lat_parts = [stacked]
    for step in (1, 2, -1, -2):
        lat_parts.append(from_behind_2(stacked, "lat", step))
    grid = jnp.stack(lat_parts, 1)
    received = grid.reshape(rows, -1, width)
    readable = jnp.concatenate([sub, received], axis=1)
    gathered = readable[:, neighbours[0, 0], :]
    result = jnp.einsum(
        "rkjc,kjcd->rkd", gathered, conv_weights[0, 0], preferred_element_type=jnp.float32
    )
    return result.astype(jnp.bfloat16).reshape(members, levels, 1, 1, -1)


def solution(mesh):
    return jax.shard_map(
        body,
        mesh=mesh,
        in_specs=(
            P("groups", "lev", "lat", "lon", None),
            P("lat", "lon", None, None, None, None),
            P("lat", "lon", None, None),
            P("lat", "lon", None),
            P("lat", "lon"),
            P("lat", "lon", None, None, None, None),
            P("lat", "lon", None, None),
        ),
        out_specs=P("groups", "lev", "lat", "lon", None),
        check_vma=False,
    )
```

profile of v0, /device:TPU:0, one launch (start us, length us, event | category | flops | bytes accessed | tf_op | source)
XLA Modules:
  0.0 107.1 jit_solution(565694133228722711)
XLA Ops:
  0.0 0.0 copy-start
  0.8 0.7 fusion.9
  1.5 0.7 compare_select_fusion.1
  2.2 0.1 copy.13
  2.2 0.1 reshape.109
  2.3 0.7 compare_select_fusion
  3.0 0.1 reshape.125
  3.1 0.0 copy-start.2
  3.1 1.5 %copy.19 = bf16[64,8,8,128]{3,2,1,0:T(8,128)(2,1)S(1)} copy(bf16[64,8,8,128]{3,1,2,0:T(8,128)(2,1)} %bitcast.75) | data formatting | bytes 2097152
  4.7 1.1 %copy.14 = bf16[512,8,128]{2,0,1:T(8,128)(2,1)} copy(bf16[512,8,128]{2,1,0:T(8,128)(2,1)S(1)} %bitcast.72) | data formatting | bytes 2097152 | tf_op jit(solution)/shard_map/reshape | solution.py:26
  5.8 3.4 %gather_fusion = bf16[16,512,128]{2,1,0:T(8,128)(2,1)} fusion(bf16[512,8,128]{2,0,1:T(8,128)(2,1)} %copy.14, s32[1024]{0:T(1024)S(1)} %pad_clamp_fusion.2), kind=kCustom, calls=%fused_computation | custom fusion | bytes 4194368 | tf_op jit(solution)/shard_map/gather | solution.py:27
  9.2 0.0 copy-done.2
  9.2 3.3 %fusion.7 = bf16[512,8,128]{2,0,1:T(8,128)(2,1)} fusion(bf16[512,8,2,128]{3,0,2,1:T(8,128)(2,1)} %bitcast.70, bf16[1,1,8,2,128,128]{5,4,3,2,1,0:T(8,128)(2,1)S(1)} %copy-done.2), kind=kOutput, calls=%fused_computation.9 | convolution fusion | flops 268959744 | bytes 3670016 | tf_op jit(solution)/shard_map/rkqc,kqcd->rkd/dot_general | solution.py:28
  12.5 1.8 %gather_fusion.1 = bf16[2,512,128]{2,1,0:T(8,128)(2,1)S(1)} fusion(bf16[512,8,128]{2,0,1:T(8,128)(2,1)} %fusion.7, s32[1024]{0:T(1024)S(1)} %get-tuple-element.6), kind=kCustom, calls=%fused_computation.1 | custom fusion | bytes 524296 | tf_op jit(solution)/shard_map/gather | solution.py:33
  14.3 0.1 bitcast_select_fusion.1
  14.4 3.0 %collective-permute-start = (bf16[512,2,128]{2,0,1:T(8,128)(2,1)S(1)}, bf16[512,2,128]{2,0,1:T(8,128)(2,1)S(1)}, u32[]{:S(2)}, u32[]{:S(2)}) collective-permute-start(bf16[512,2,128]{2,0,1:T(8,128)(2,1)S(1)} %bitcast_select_fusion.1), channel_id=1, source_target_pairs={{2,0},{0,2},{3,1},{1,3},{6,4},{4,6},{7,5},{5,7},{10,8},{8,10},{11,... | collective-permute-start | bytes 786440 | tf_op jit(solution)/shard_map/ppermute | solution.py:10
  17.4 0.1 bitcast_select_fusion
  17.5 6.2 %collective-permute-done = bf16[512,2,128]{2,0,1:T(8,128)(2,1)S(1)} collective-permute-done((bf16[512,2,128]{2,0,1:T(8,128)(2,1)S(1)}, bf16[512,2,128]{2,0,1:T(8,128)(2,1)S(1)}, u32[]{:S(2)}, u32[]{:S(2)}) %collective-permute-start) | collective-permute-done | bytes 262176 | tf_op jit(solution)/shard_map/ppermute | solution.py:10
  23.7 0.1 pad_maximum_fusion.1
  23.8 0.0 copy-start.1
  23.8 3.9 %collective-permute-start.1 = (bf16[512,3,2,128]{3,0,2,1:T(8,128)(2,1)S(1)}, bf16[512,3,2,128]{3,0,2,1:T(8,128)(2,1)S(1)}, u32[]{:S(2)}, u32[]{:S(2)}) collective-permute-start(bf16[512,3,2,128]{3,0,2,1:T(8,128)(2,1)S(1)} %pad_maximum_fusion.1), channel_id=1, source_target_pairs={{0,4},{4,8},{8,12},{1,5},{5,9},{9,13},{2,6},{6,10},{10,14},{3,7},{... | collective-permute-start | bytes 2359304 | tf_op jit(solution)/shard_map/ppermute | solution.py:16
  27.7 4.5 %collective-permute-start.2 = (bf16[512,3,2,128]{3,0,2,1:T(8,128)(2,1)S(1)}, bf16[512,3,2,128]{3,0,2,1:T(8,128)(2,1)S(1)}, u32[]{:S(2)}, u32[]{:S(2)}) collective-permute-start(bf16[512,3,2,128]{3,0,2,1:T(8,128)(2,1)S(1)} %pad_maximum_fusion.1), channel_id=1, source_target_pairs={{0,8},{4,12},{1,9},{5,13},{2,10},{6,14},{3,11},{7,15},{16,24},{20,... | collective-permute-start | bytes 2359304 | tf_op jit(solution)/shard_map/ppermute | solution.py:16
  32.2 1.3 %collective-permute-start.3 = (bf16[512,3,2,128]{3,0,2,1:T(8,128)(2,1)S(1)}, bf16[512,3,2,128]{3,0,2,1:T(8,128)(2,1)S(1)}, u32[]{:S(2)}, u32[]{:S(2)}) collective-permute-start(bf16[512,3,2,128]{3,0,2,1:T(8,128)(2,1)S(1)} %pad_maximum_fusion.1), channel_id=1, source_target_pairs={{4,0},{8,4},{12,8},{5,1},{9,5},{13,9},{6,2},{10,6},{14,10},{7,3},{... | collective-permute-start | bytes 2359304 | tf_op jit(solution)/shard_map/ppermute | solution.py:16
  33.5 1.3 %collective-permute-start.4 = (bf16[512,3,2,128]{3,0,2,1:T(8,128)(2,1)S(1)}, bf16[512,3,2,128]{3,0,2,1:T(8,128)(2,1)S(1)}, u32[]{:S(2)}, u32[]{:S(2)}) collective-permute-start(bf16[512,3,2,128]{3,0,2,1:T(8,128)(2,1)S(1)} %pad_maximum_fusion.1), channel_id=1, source_target_pairs={{8,0},{12,4},{9,1},{13,5},{10,2},{14,6},{11,3},{15,7},{24,16},{28,... | collective-permute-start | bytes 2359304 | tf_op jit(solution)/shard_map/ppermute | solution.py:16
  34.8 0.1 bitcast_dynamic-update-slice_fusion.4
  34.9 10.7 %collective-permute-done.1 = bf16[512,3,2,128]{3,0,2,1:T(8,128)(2,1)S(1)} collective-permute-done((bf16[512,3,2,128]{3,0,2,1:T(8,128)(2,1)S(1)}, bf16[512,3,2,128]{3,0,2,1:T(8,128)(2,1)S(1)}, u32[]{:S(2)}, u32[]{:S(2)}) %collective-permute-start.1) | collective-permute-done | bytes 786464 | tf_op jit(solution)/shard_map/ppermute | solution.py:16
  45.6 0.1 bitcast_dynamic-update-slice_fusion.3
  45.8 14.7 %collective-permute-done.2 = bf16[512,3,2,128]{3,0,2,1:T(8,128)(2,1)S(1)} collective-permute-done((bf16[512,3,2,128]{3,0,2,1:T(8,128)(2,1)S(1)}, bf16[512,3,2,128]{3,0,2,1:T(8,128)(2,1)S(1)}, u32[]{:S(2)}, u32[]{:S(2)}) %collective-permute-start.2) | collective-permute-done | bytes 786464 | tf_op jit(solution)/shard_map/ppermute | solution.py:16
  60.5 0.1 bitcast_dynamic-update-slice_fusion.2
  60.6 0.0 collective-permute-done.3
  60.6 0.1 bitcast_dynamic-update-slice_fusion.1
  60.7 24.1 %collective-permute-done.4 = bf16[512,3,2,128]{3,0,2,1:T(8,128)(2,1)S(1)} collective-permute-done((bf16[512,3,2,128]{3,0,2,1:T(8,128)(2,1)S(1)}, bf16[512,3,2,128]{3,0,2,1:T(8,128)(2,1)S(1)}, u32[]{:S(2)}, u32[]{:S(2)}) %collective-permute-start.4) | collective-permute-done | bytes 786464 | tf_op jit(solution)/shard_map/ppermute | solution.py:16
  84.8 0.1 bitcast_dynamic-update-slice_fusion
  84.9 0.0 copy-done.1
  84.9 2.7 %pad_maximum_fusion = bf16[512,38,128]{2,0,1:T(8,128)(2,1)} fusion(bf16[512,30,128]{2,0,1:T(8,128)(2,1)S(1)} %bitcast.71, bf16[512,8,128]{2,0,1:T(8,128)(2,1)S(1)} %copy-done.1), kind=kLoop, calls=%fused_computation.3 | loop fusion | flops 2490368 | bytes 9961472 | tf_op jit(solution)/shard_map/concatenate | solution.py:43
  87.6 8.7 %gather_fusion.2 = bf16[80,512,128]{2,1,0:T(8,128)(2,1)} fusion(bf16[512,38,128]{2,0,1:T(8,128)(2,1)} %pad_maximum_fusion, s32[1024]{0:T(1024)S(1)} %get-tuple-element.5), kind=kCustom, calls=%fused_computation.2 | custom fusion | bytes 20971840 | tf_op jit(solution)/shard_map/gather | solution.py:44
  96.3 0.0 copy-done
  96.3 6.8 %fusion.4 = bf16[512,8,128]{2,0,1:T(8,128)(2,1)S(1)} fusion(bf16[512,8,10,128]{3,0,2,1:T(8,128)(2,1)} %bitcast.69, bf16[1,1,8,10,128,128]{5,4,3,2,1,0:T(8,128)(2,1)S(1)} %copy-done), kind=kOutput, calls=%fused_computation.8 | convolution fusion | flops 1342701568 | bytes 14155776 | tf_op jit(solution)/shard_map/rkjc,kjcd->rkd/dot_general | solution.py:45
  103.2 1.6 %copy.15 = bf16[512,8,128]{2,1,0:T(8,128)(2,1)} copy(bf16[512,8,128]{2,0,1:T(8,128)(2,1)S(1)} %fusion.4) | data formatting | bytes 2097152 | tf_op jit(solution)/shard_map/convert_element_type | solution.py:48
  104.8 2.3 %reshape.106 = bf16[8,64,1,1,1024]{4,1,0,3,2:T(8,128)(2,1)} reshape(bf16[512,8,128]{2,1,0:T(8,128)(2,1)} %copy.15) | data formatting | bytes 2097152 | tf_op jit(solution)/shard_map/reshape | solution.py:48
  (3 shorter events, 0.0 us)
Async XLA Ops:
  0.0 96.3 %copy-start = (bf16[1,1,8,10,128,128]{5,4,3,2,1,0:T(8,128)(2,1)S(1)}, bf16[1,1,8,10,128,128]{5,4,3,2,1,0:T(8,128)(2,1)}, u32[]{:S(2)}) copy-start(bf16[1,1,8,10,128,128]{5,4,3,2,1,0:T(8,128)(2,1)} %param.12) | copy-start | bytes 7864324
  3.1 6.1 %copy-start.2 = (bf16[1,1,8,2,128,128]{5,4,3,2,1,0:T(8,128)(2,1)S(1)}, bf16[1,1,8,2,128,128]{5,4,3,2,1,0:T(8,128)(2,1)}, u32[]{:S(2)}) copy-start(bf16[1,1,8,2,128,128]{5,4,3,2,1,0:T(8,128)(2,1)} %param.8) | copy-start | bytes 1572868
  14.4 9.3 %collective-permute-start = (bf16[512,2,128]{2,0,1:T(8,128)(2,1)S(1)}, bf16[512,2,128]{2,0,1:T(8,128)(2,1)S(1)}, u32[]{:S(2)}, u32[]{:S(2)}) collective-permute-start(bf16[512,2,128]{2,0,1:T(8,128)(2,1)S(1)} %bitcast_select_fusion.1), channel_id=1, source_target_pairs={{2,0},{0,2},{3,1},{1,3},{6,4},{4,6},{7,5},{5,7},{10,8},{8,10},{11,... | collective-permute-start | bytes 786440 | tf_op jit(solution)/shard_map/ppermute | solution.py:10
  23.8 61.1 %copy-start.1 = (bf16[512,8,128]{2,0,1:T(8,128)(2,1)S(1)}, bf16[512,8,128]{2,0,1:T(8,128)(2,1)}, u32[]{:S(2)}) copy-start(bf16[512,8,128]{2,0,1:T(8,128)(2,1)} %fusion.7) | copy-start | bytes 3145732
  23.8 21.8 %collective-permute-start.1 = (bf16[512,3,2,128]{3,0,2,1:T(8,128)(2,1)S(1)}, bf16[512,3,2,128]{3,0,2,1:T(8,128)(2,1)S(1)}, u32[]{:S(2)}, u32[]{:S(2)}) collective-permute-start(bf16[512,3,2,128]{3,0,2,1:T(8,128)(2,1)S(1)} %pad_maximum_fusion.1), channel_id=1, source_target_pairs={{0,4},{4,8},{8,12},{1,5},{5,9},{9,13},{2,6},{6,10},{10,14},{3,7},{... | collective-permute-start | bytes 2359304 | tf_op jit(solution)/shard_map/ppermute | solution.py:16
  27.7 32.8 %collective-permute-start.2 = (bf16[512,3,2,128]{3,0,2,1:T(8,128)(2,1)S(1)}, bf16[512,3,2,128]{3,0,2,1:T(8,128)(2,1)S(1)}, u32[]{:S(2)}, u32[]{:S(2)}) collective-permute-start(bf16[512,3,2,128]{3,0,2,1:T(8,128)(2,1)S(1)} %pad_maximum_fusion.1), channel_id=1, source_target_pairs={{0,8},{4,12},{1,9},{5,13},{2,10},{6,14},{3,11},{7,15},{16,24},{20,... | collective-permute-start | bytes 2359304 | tf_op jit(solution)/shard_map/ppermute | solution.py:16
  32.2 28.4 %collective-permute-start.3 = (bf16[512,3,2,128]{3,0,2,1:T(8,128)(2,1)S(1)}, bf16[512,3,2,128]{3,0,2,1:T(8,128)(2,1)S(1)}, u32[]{:S(2)}, u32[]{:S(2)}) collective-permute-start(bf16[512,3,2,128]{3,0,2,1:T(8,128)(2,1)S(1)} %pad_maximum_fusion.1), channel_id=1, source_target_pairs={{4,0},{8,4},{12,8},{5,1},{9,5},{13,9},{6,2},{10,6},{14,10},{7,3},{... | collective-permute-start | bytes 2359304 | tf_op jit(solution)/shard_map/ppermute | solution.py:16
  33.5 51.2 %collective-permute-start.4 = (bf16[512,3,2,128]{3,0,2,1:T(8,128)(2,1)S(1)}, bf16[512,3,2,128]{3,0,2,1:T(8,128)(2,1)S(1)}, u32[]{:S(2)}, u32[]{:S(2)}) collective-permute-start(bf16[512,3,2,128]{3,0,2,1:T(8,128)(2,1)S(1)} %pad_maximum_fusion.1), channel_id=1, source_target_pairs={{8,0},{12,4},{9,1},{13,5},{10,2},{14,6},{11,3},{15,7},{24,16},{28,... | collective-permute-start | bytes 2359304 | tf_op jit(solution)/shard_map/ppermute | solution.py:16
where the time goes:
time: 108 us; the launch traced here: 107 us
  waiting for transfers between devices  55.7 us (52%)
  local copies, waits for them, and re-layouts  21.2 us (20%)
  starting transfers between devices  14 us (13%)
  matrix products  10.1 us (9%)
  other arithmetic  5.12 us (5%)
    ppermute x4, waiting for transfers between devices, from_behind_2(): return lax.ppermute(shard, axis, pairs)  49.5 us
    ppermute x4, starting transfers between devices, from_behind_2(): return lax.ppermute(shard, axis, pairs)  11 us
    gather x1, local copies, waits for them, and re-layouts, body(): gathered = readable[:, neighbours[0, 0], :]  8.7 us
    dot_general x1, matrix products, body(): jnp.einsum('rkjc,kjcd->rkd', gathered, conv_weights[0, 0], preferred_elem...  6.84 us
    ppermute x1, waiting for transfers between devices, from_behind(): return lax.ppermute(block, axis, route)  6.21 us
    gather x1, local copies, waits for them, and re-layouts, body(): picked = cells[:, interp_blocks[0, 0], :]  3.38 us
    dot_general x1, matrix products, body(): jnp.einsum('rkqc,kqcd->rkd', picked, interp_weights[0, 0], preferred_elem...  3.27 us
    ppermute x1, starting transfers between devices, from_behind(): return lax.ppermute(block, axis, route)  3 us
  transfers between devices with their start and end apart: 5, of which 4 were waited for; matrix products, arithmetic and copies ran while one was open for 0% of the time, Pallas kernels for 0%

commit v1 on v0

v1 whole, which is shorter than its diff:
```python
import functools

import jax
import jax.numpy as jnp
from jax import lax
from jax.experimental import pallas as pl
from jax.experimental.pallas import tpu as pltpu
from jax.sharding import PartitionSpec as P

MESH = pl.DeviceIdType.MESH
STEPS = (0, 1, 2, -1, -2)
CHUNKS = 4


def kernel(
    n_lat,
    n_lon,
    sides,
    blocks_ref,
    list_ref,
    count_ref,
    near_ref,
    field_hbm,
    interp_hbm,
    conv_hbm,
    out_hbm,
    field,
    interp,
    conv,
    out,
    field_sem,
    weight_sem,
    out_sem,
    send_sem,
    recv_sem,
    *readable,
):
    chunks = len(readable)
    width = interp.shape[-1]
    tiles = interp.shape[0]
    joins = conv.shape[1] // width
    feeds = interp.shape[1] // width
    slots = list_ref.shape[1]
    rows = field.shape[1] // chunks
    spots = 1 + len(sides)
    lat, lon = lax.axis_index("lat"), lax.axis_index("lon")

    loads = [pltpu.make_async_copy(interp_hbm, interp, weight_sem.at[0])]
    for k in range(field.shape[0]):
        columns = pl.ds(k * width, width)
        loads.append(
            pltpu.make_async_copy(field_hbm.at[:, columns], field.at[k], field_sem.at[k])
        )
    conv_load = pltpu.make_async_copy(conv_hbm, conv, weight_sem.at[1])
    for load in loads:
        load.start()
    conv_load.start()

    def inside(band):
        return jnp.logical_and(band >= 0, band < n_lat)

    def beside(step):
        return lax.rem(lon + step + n_lon, n_lon)

    def lon_first(source, a):
        if a == 1:
            return source == 0
        if a == -1:
            return source == n_lat - 1
        return False

    barrier = pltpu.get_barrier_semaphore()
    for a in STEPS[1:]:

        @pl.when(inside(lat + a))
        def _():
            pl.semaphore_signal(barrier, 1, device_id={"lat": lat + a}, device_id_type=MESH)

    for b in sides:
        pl.semaphore_signal(barrier, 1, device_id={"lon": beside(b)}, device_id_type=MESH)

    def slot(ai, p):
        return pl.ds(tiles + (ai * spots + p) * slots, slots)

    zeros = jnp.zeros((spots * slots, rows, width), jnp.bfloat16)
    for ai, a in enumerate(STEPS):
        if a:

            @pl.when(jnp.logical_not(inside(lat - a)))
            def _():
                for c in range(chunks):
                    readable[c][pl.ds(tiles + ai * spots * slots, spots * slots)] = zeros

    def interpolated(c, k):
        picked = [
            field[blocks_ref[q, k], pl.ds(c * rows, rows)]
            for q in range(feeds)
        ]
        return jnp.dot(
            jnp.concatenate(picked, axis=1), interp[k], preferred_element_type=jnp.float32
        ).astype(jnp.bfloat16)

    def transfer(c, flow, from_ai, from_p, to_ai, to_p, target):
        return pltpu.make_async_remote_copy(
            src_ref=readable[c].at[slot(from_ai, from_p)],
            dst_ref=readable[c].at[slot(to_ai, to_p)],
            send_sem=send_sem.at[flow, c],
            recv_sem=recv_sem.at[to_ai * spots + to_p, c],
            device_id=target,
            device_id_type=MESH,
        )

    def along_lat(c, ai):
        return transfer(c, ai, 0, 0, ai, 0, {"lat": lat + STEPS[ai]})

    def along_lon(c, p):
        return transfer(c, 5 * p, 0, 0, 0, p, {"lon": beside(sides[p - 1])})

    def lat_then_lon(c, ai, p):
        return transfer(c, 5 * p + ai, ai, 0, ai, p, {"lon": beside(sides[p - 1])})

    def lon_then_lat(c, ai, p):
        return transfer(c, 5 * spots + 5 * (p - 1) + ai, 0, p, ai, p, {"lat": lat + STEPS[ai]})

    def received(c, ai, p):
        return transfer(c, 0, ai, p, ai, p, {"lon": beside(1)})

    order = (1, 3, 2, 4)
    for load in loads:
        load.wait()
    for c in range(chunks):
        for h in range(slots):
            value = interpolated(c, list_ref[0, h])
            live = h < jnp.full(value.shape, count_ref[0, 0])
            readable[c][tiles + h] = jnp.where(live, value, jnp.zeros_like(value))
        if c == 0:
            peers = len(sides) + sum(inside(lat + a).astype(jnp.int32) for a in STEPS[1:])
            pl.semaphore_wait(barrier, peers)
        for p in range(1, spots):
            along_lon(c, p).start()
        for ai in order:

            @pl.when(inside(lat + STEPS[ai]))
            def _():
                along_lat(c, ai).start()

    def place(k, n):
        e = near_ref[k, n]
        if spots == 2:
            t = jnp.maximum(e - tiles, 0)
            group = t * 43 // 256
            r = t - group * (3 * slots)
            far = tiles + group * (2 * slots) + r - jnp.where(r >= 2 * slots, slots, 0)
            e = jnp.where(e < tiles, e, far)
        return e

    for c in range(chunks):
        for k in range(tiles):
            readable[c][k] = interpolated(c, k)

    def forward(c):
        for p in range(1, spots):
            received(c, 0, p).wait_recv()
            for ai in (1, 3):

                @pl.when(jnp.logical_and(inside(lat + STEPS[ai]), lon_first(lat, STEPS[ai])))
                def _():
                    lon_then_lat(c, ai, p).start()

        for ai in order:
            a = STEPS[ai]

            @pl.when(inside(lat - a))
            def _():
                received(c, ai, 0).wait_recv()

            @pl.when(jnp.logical_and(inside(lat - a), jnp.logical_not(lon_first(lat - a, a))))
            def _():
                for p in range(1, spots):
                    lat_then_lon(c, ai, p).start()

    def convolve(c):
        for ai in order:

            @pl.when(inside(lat - STEPS[ai]))
            def _():
                for p in range(1, spots):
                    received(c, ai, p).wait_recv()

        part = pl.ds(c * rows, rows)
        for k in range(tiles):
            gathered = jnp.concatenate(
                [readable[c][place(k, n)] for n in range(joins)], axis=1
            )
            out[part, k * width : (k + 1) * width] = jnp.dot(
                gathered, conv[k], preferred_element_type=jnp.float32
            ).astype(jnp.bfloat16)
        pltpu.make_async_copy(out.at[part], out_hbm.at[part], out_sem.at[c]).start()

    for c in range(chunks):
        forward(c)
        if c == 0:
            conv_load.wait()
        else:
            convolve(c - 1)
    convolve(chunks - 1)

    for c in range(chunks):
        for p in range(1, spots):
            along_lon(c, p).wait_send()
        for ai in order:
            a = STEPS[ai]

            @pl.when(inside(lat + a))
            def _():
                along_lat(c, ai).wait_send()

            if abs(a) == 1:

                @pl.when(jnp.logical_and(inside(lat + a), lon_first(lat, a)))
                def _():
                    for p in range(1, spots):
                        lon_then_lat(c, ai, p).wait_send()

            @pl.when(jnp.logical_and(inside(lat - a), jnp.logical_not(lon_first(lat - a, a))))
            def _():
                for p in range(1, spots):
                    lat_then_lon(c, ai, p).wait_send()

        part = pl.ds(c * rows, rows)
        pltpu.make_async_copy(out.at[part], out_hbm.at[part], out_sem.at[c]).wait()


def body(
    n_lat,
    n_lon,
    model_field,
    interp_weights,
    interp_blocks,
    send_list,
    send_count,
    conv_weights,
    neighbours,
):
    members, levels = model_field.shape[:2]
    tiles, feeds, width = interp_weights.shape[2:5]
    joins, slots = conv_weights.shape[3], send_list.shape[2]
    rows = members * levels
    cells = model_field.shape[-1]
    sides = (1,) if n_lon == 2 else (1, -1)
    spots = 1 + len(sides)
    smem = pl.BlockSpec(memory_space=pltpu.SMEM)
    whole = pl.BlockSpec(memory_space=pl.ANY)
    flops = 2 * rows * width * width * tiles * (feeds + joins)
    result = pl.pallas_call(
        functools.partial(kernel, n_lat, n_lon, sides),
        out_shape=jax.ShapeDtypeStruct((rows, tiles * width), jnp.bfloat16),
        in_specs=[smem] * 4 + [whole] * 3,
        out_specs=whole,
        scratch_shapes=[
            pltpu.VMEM((cells // width, rows, width), jnp.bfloat16),
            pltpu.VMEM((tiles, feeds * width, width), jnp.bfloat16),
            pltpu.VMEM((tiles, joins * width, width), jnp.bfloat16),
            pltpu.VMEM((rows, tiles * width), jnp.bfloat16),
            pltpu.SemaphoreType.DMA((cells // width,)),
            pltpu.SemaphoreType.DMA((2,)),
            pltpu.SemaphoreType.DMA((CHUNKS,)),
            pltpu.SemaphoreType.DMA((5 * (2 * spots - 1), CHUNKS)),
            pltpu.SemaphoreType.DMA((5 * spots, CHUNKS)),
        ]
        + [
            pltpu.VMEM((tiles + 5 * spots * slots, rows // CHUNKS, width), jnp.bfloat16)
            for _ in range(CHUNKS)
        ],
        compiler_params=pltpu.CompilerParams(
            collective_id=0, has_side_effects=True, vmem_limit_bytes=32 * 1024 * 1024
        ),
        cost_estimate=pl.CostEstimate(
            flops=flops, bytes_accessed=6 * 1024 * 1024, transcendentals=0
        ),
    )(
        interp_blocks[0, 0].T,
        send_list[0],
        send_count,
        neighbours[0, 0],
        model_field.reshape(rows, cells),
        interp_weights.reshape(tiles, feeds * width, width),
        conv_weights.reshape(tiles, joins * width, width),
    )
    return result.reshape(members, levels, 1, 1, -1)


def solution(mesh):
    return jax.shard_map(
        functools.partial(body, mesh.shape["lat"], mesh.shape["lon"]),
        mesh=mesh,
        in_specs=(
            P("groups", "lev", "lat", "lon", None),
            P("lat", "lon", None, None, None, None),
            P("lat", "lon", None, None),
            P("lat", "lon", None),
            P("lat", "lon"),
            P("lat", "lon", None, None, None, None),
            P("lat", "lon", None, None),
        ),
        out_specs=P("groups", "lev", "lat", "lon", None),
        check_vma=False,
    )
```

time: 108 us -> 38.1 us (0.35)
  waiting for transfers between devices: 55.7 us -> 0 us
  Pallas kernels: 0 us -> 30.1 us
  local copies, waits for them, and re-layouts: 21.2 us -> 6.99 us
  starting transfers between devices: 14 us -> 0 us
  matrix products: 10.1 us -> 0 us
  other arithmetic: 5.12 us -> 0 us
    ppermute x5 -> x0, waiting for transfers between devices: 55.7 us -> none  [the longest x4 49.5 us: from_behind_2(): return lax.ppermute(shard, axis, pairs)]
    pallas_call x0 -> x1, Pallas kernels: none -> 30.1 us  [body(): pl.pallas_call(functools.partial(kernel, n_lat, n_lon, sides), out_shape=...]
    ppermute x5 -> x0, starting transfers between devices: 14 us -> none  [the longest x4 11 us: from_behind_2(): return lax.ppermute(shard, axis, pairs)]
    gather x3 -> x0, local copies, waits for them, and re-layouts: 13.9 us -> none  [the longest x1 8.7 us: body(): gathered = readable[:, neighbours[0, 0], :]]
    dot_general x2 -> x0, matrix products: 10.1 us -> none  [the longest x1 6.84 us: body(): jnp.einsum('rkjc,kjcd->rkd', gathered, conv_weights[0, 0], preferred_elem...]
    unnamed x10 -> x13, local copies, waits for them, and re-layouts: 1.87 us -> 6.99 us
    reshape x2 -> x0, local copies, waits for them, and re-layouts: 3.44 us -> none  [the longest x1 2.29 us: body(): return result.astype(jnp.bfloat16).reshape(members, levels, 1, 1, -1)]
    concatenate x1 -> x0, other arithmetic: 2.72 us -> none  [body(): readable = jnp.concatenate([sub, received], axis=1)]
  transfers between devices with their start and end apart: 5 -> 0, of which waited for: 4 -> 0; matrix products, arithmetic and copies ran while one was open for 0% -> 0% of each run, Pallas kernels for 0% -> 0%
where the time goes in v1:
time: 38.1 us; the launch traced here: 37.8 us
  Pallas kernels  30.1 us (79%)
  local copies, waits for them, and re-layouts  6.99 us (18%)
  between operations  0.67 us (2%)
    pallas_call x1, Pallas kernels, body(): pl.pallas_call(functools.partial(kernel, n_lat, n_lon, sides), out_shape=...  30.1 us
    unnamed x13, local copies, waits for them, and re-layouts  6.99 us

profile of v1, /device:TPU:0, one launch (start us, length us, event | category | flops | bytes accessed | tf_op | source)
XLA Modules:
  0.0 37.8 jit_solution(2329144198576186605)
XLA Ops:
  0.7 0.0 copy-start
  0.7 1.7 %copy-done = bf16[1,1,8,10,128,128]{5,4,3,2,1,0:T(8,128)(2,1)S(1)} copy-done((bf16[1,1,8,10,128,128]{5,4,3,2,1,0:T(8,128)(2,1)S(1)}, bf16[1,1,8,10,128,128]{5,4,3,2,1,0:T(8,128)(2,1)}, u32[]{:S(2)}) %copy-start) | copy-done | bytes 2621464
  2.4 0.0 copy-start.1
  2.4 1.2 %copy-done.1 = bf16[8,64,1,1,1024]{4,1,3,2,0:T(8,128)(2,1)S(1)} copy-done((bf16[8,64,1,1,1024]{4,1,3,2,0:T(8,128)(2,1)S(1)}, bf16[8,64,1,1,1024]{4,1,3,2,0:T(8,128)(2,1)}, u32[]{:S(2)}) %copy-start.1) | copy-done | bytes 1048600
  3.6 0.0 copy-start.2
  3.6 1.0 %copy-done.2 = bf16[1,1,8,2,128,128]{5,4,3,2,1,0:T(8,128)(2,1)S(1)} copy-done((bf16[1,1,8,2,128,128]{5,4,3,2,1,0:T(8,128)(2,1)S(1)}, bf16[1,1,8,2,128,128]{5,4,3,2,1,0:T(8,128)(2,1)}, u32[]{:S(2)}) %copy-start.2) | copy-done | bytes 524312
  4.7 0.0 copy-start.3
  4.7 0.7 %copy-done.3 = s32[1,1,8,10]{3,2,1,0:T(8,128)S(1)} copy-done((s32[1,1,8,10]{3,2,1,0:T(8,128)S(1)}, s32[1,1,8,10]{3,2,1,0:T(8,128)}, u32[]{:S(2)}) %copy-start.3) | copy-done | bytes 344
  5.3 0.0 copy-start.4
  5.3 0.7 %copy-done.4 = s32[1,1,8,2]{2,3,1,0:T(2,128)S(1)} copy-done((s32[1,1,8,2]{2,3,1,0:T(2,128)S(1)}, s32[1,1,8,2]{2,3,1,0:T(2,128)}, u32[]{:S(2)}) %copy-start.4) | copy-done | bytes 88
  6.0 0.0 copy-start.5
  6.0 0.7 %copy-done.5 = s32[1,1,2]{2,1,0:T(1,128)S(1)} copy-done((s32[1,1,2]{2,1,0:T(1,128)S(1)}, s32[1,1,2]{2,1,0:T(1,128)}, u32[]{:S(2)}) %copy-start.5) | copy-done | bytes 32
  6.7 30.1 %shard_map.73 = bf16[512,1024]{1,0:T(8,128)(2,1)S(1)} custom-call(s32[2,8]{1,0:T(2,128)S(1)} %bitcast.16, s32[1,2]{1,0:T(1,128)S(1)} %bitcast.17, s32[1,1]{1,0:T(1,128)S(6)} %copy.10.count_ref, s32[8,10]{1,0:T(8,128)S(1)} %bitcast.15, bf16[512,1024]{1,0:T(8,128)(2,1)S(1)} %bitcast.13, bf16[8,256,128]{2,1,0:T(8,128)(2,1)S(1)} %bitcast.14, ...), custom_call_target="tpu_custom_call" | custom-call | flops 1610612736 | bytes 6291456 | tf_op jit(solution)/shard_map/pallas_call | solution.py:255
  36.8 1.0 %copy.11 = bf16[8,64,1,1,1024]{4,1,3,2,0:T(8,128)(2,1)} copy(bf16[8,64,1,1,1024]{4,1,3,2,0:T(8,128)(2,1)S(1)} %bitcast.11) | data formatting | bytes 2097152
Async XLA Ops:
  0.7 1.7 %copy-start = (bf16[1,1,8,10,128,128]{5,4,3,2,1,0:T(8,128)(2,1)S(1)}, bf16[1,1,8,10,128,128]{5,4,3,2,1,0:T(8,128)(2,1)}, u32[]{:S(2)}) copy-start(bf16[1,1,8,10,128,128]{5,4,3,2,1,0:T(8,128)(2,1)} %param.12) | copy-start | bytes 7864324
  2.4 1.2 %copy-start.1 = (bf16[8,64,1,1,1024]{4,1,3,2,0:T(8,128)(2,1)S(1)}, bf16[8,64,1,1,1024]{4,1,3,2,0:T(8,128)(2,1)}, u32[]{:S(2)}) copy-start(bf16[8,64,1,1,1024]{4,1,3,2,0:T(8,128)(2,1)} %param.7) | copy-start | bytes 3145732
  3.6 1.0 %copy-start.2 = (bf16[1,1,8,2,128,128]{5,4,3,2,1,0:T(8,128)(2,1)S(1)}, bf16[1,1,8,2,128,128]{5,4,3,2,1,0:T(8,128)(2,1)}, u32[]{:S(2)}) copy-start(bf16[1,1,8,2,128,128]{5,4,3,2,1,0:T(8,128)(2,1)} %param.8) | copy-start | bytes 1572868
  4.7 0.7 %copy-start.3 = (s32[1,1,8,10]{3,2,1,0:T(8,128)S(1)}, s32[1,1,8,10]{3,2,1,0:T(8,128)}, u32[]{:S(2)}) copy-start(s32[1,1,8,10]{3,2,1,0:T(8,128)} %param.13) | copy-start | bytes 964
  5.3 0.7 %copy-start.4 = (s32[1,1,8,2]{2,3,1,0:T(2,128)S(1)}, s32[1,1,8,2]{2,3,1,0:T(2,128)}, u32[]{:S(2)}) copy-start(s32[1,1,8,2]{2,3,1,0:T(2,128)} %param.9) | copy-start | bytes 196
  6.0 0.7 %copy-start.5 = (s32[1,1,2]{2,1,0:T(1,128)S(1)}, s32[1,1,2]{2,1,0:T(1,128)}, u32[]{:S(2)}) copy-start(s32[1,1,2]{2,1,0:T(1,128)} %param.10) | copy-start | bytes 28

commit v2 on v1

--- a/solution.py
+++ b/solution.py
@@ -9,7 +9,7 @@
 
 MESH = pl.DeviceIdType.MESH
 STEPS = (0, 1, 2, -1, -2)
-CHUNKS = 4
+CHUNKS = 2
 
 
 def kernel(
@@ -23,14 +23,12 @@
     field_hbm,
     interp_hbm,
     conv_hbm,
-    out_hbm,
+    out,
     field,
     interp,
     conv,
-    out,
     field_sem,
     weight_sem,
-    out_sem,
     send_sem,
     recv_sem,
     *readable,
@@ -70,7 +68,7 @@
         return False
 
     barrier = pltpu.get_barrier_semaphore()
-    for a in STEPS[1:]:
+    for a in (1, -1):
 
         @pl.when(inside(lat + a))
         def _():
@@ -111,7 +109,12 @@
         )
 
     def along_lat(c, ai):
-        return transfer(c, ai, 0, 0, ai, 0, {"lat": lat + STEPS[ai]})
+        near = STEPS[ai] // abs(STEPS[ai])
+        from_ai = 0 if STEPS[ai] == near else STEPS.index(near)
+        return transfer(c, ai, from_ai, 0, ai, 0, {"lat": lat + near})
+
+    def passes_on(a):
+        return jnp.logical_and(inside(lat + a), inside(lat - a))
 
     def along_lon(c, p):
         return transfer(c, 5 * p, 0, 0, 0, p, {"lon": beside(sides[p - 1])})
@@ -126,6 +129,7 @@
         return transfer(c, 0, ai, p, ai, p, {"lon": beside(1)})
 
     order = (1, 3, 2, 4)
+    near_order, far_order = order[:2], order[2:]
     for load in loads:
         load.wait()
     for c in range(chunks):
@@ -134,11 +138,11 @@
             live = h < jnp.full(value.shape, count_ref[0, 0])
             readable[c][tiles + h] = jnp.where(live, value, jnp.zeros_like(value))
         if c == 0:
-            peers = len(sides) + sum(inside(lat + a).astype(jnp.int32) for a in STEPS[1:])
+            peers = len(sides) + sum(inside(lat + a).astype(jnp.int32) for a in (1, -1))
             pl.semaphore_wait(barrier, peers)
         for p in range(1, spots):
             along_lon(c, p).start()
-        for ai in order:
+        for ai in near_order:
 
             @pl.when(inside(lat + STEPS[ai]))
             def _():
@@ -154,10 +158,6 @@
             e = jnp.where(e < tiles, e, far)
         return e
 
-    for c in range(chunks):
-        for k in range(tiles):
-            readable[c][k] = interpolated(c, k)
-
     def forward(c):
         for p in range(1, spots):
             received(c, 0, p).wait_recv()
@@ -167,17 +167,35 @@
                 def _():
                     lon_then_lat(c, ai, p).start()
 
-        for ai in order:
+        for ai in near_order:
             a = STEPS[ai]
 
             @pl.when(inside(lat - a))
             def _():
                 received(c, ai, 0).wait_recv()
 
-            @pl.when(jnp.logical_and(inside(lat - a), jnp.logical_not(lon_first(lat - a, a))))
-            def _():
-                for p in range(1, spots):
-                    lat_then_lon(c, ai, p).start()
+            @pl.when(passes_on(a))
+            def _():
+                along_lat(c, STEPS.index(2 * a)).start()
+
+            across(c, ai)
+
+    def across(c, ai):
+        a = STEPS[ai]
+
+        @pl.when(jnp.logical_and(inside(lat - a), jnp.logical_not(lon_first(lat - a, a))))
+        def _():
+            for p in range(1, spots):
+                lat_then_lon(c, ai, p).start()
+
+    def forward_far(c):
+        for ai in far_order:
+
+            @pl.when(inside(lat - STEPS[ai]))
+            def _():
+                received(c, ai, 0).wait_recv()
+
+            across(c, ai)
 
     def convolve(c):
         for ai in order:
@@ -195,15 +213,19 @@
             out[part, k * width : (k + 1) * width] = jnp.dot(
                 gathered, conv[k], preferred_element_type=jnp.float32
             ).astype(jnp.bfloat16)
-        pltpu.make_async_copy(out.at[part], out_hbm.at[part], out_sem.at[c]).start()
-
-    for c in range(chunks):
-        forward(c)
-        if c == 0:
+
+    for c in range(chunks + 2):
+        if c < chunks:
+            forward(c)
+        if 1 <= c <= chunks:
+            forward_far(c - 1)
+        if c < chunks:
+            for k in range(tiles):
+                readable[c][k] = interpolated(c, k)
+        if c == 1:
             conv_load.wait()
-        else:
-            convolve(c - 1)
-    convolve(chunks - 1)
+        if c >= 2:
+            convolve(c - 2)
 
     for c in range(chunks):
         for p in range(1, spots):
@@ -211,7 +233,7 @@
         for ai in order:
             a = STEPS[ai]
 
-            @pl.when(inside(lat + a))
+            @pl.when(inside(lat + a) if abs(a) == 1 else passes_on(a // 2))
             def _():
                 along_lat(c, ai).wait_send()
 
@@ -226,9 +248,6 @@
             def _():
                 for p in range(1, spots):
                     lat_then_lon(c, ai, p).wait_send()
-
-        part = pl.ds(c * rows, rows)
-        pltpu.make_async_copy(out.at[part], out_hbm.at[part], out_sem.at[c]).wait()
 
 
 def body(
@@ -250,21 +269,19 @@
     sides = (1,) if n_lon == 2 else (1, -1)
     spots = 1 + len(sides)
     smem = pl.BlockSpec(memory_space=pltpu.SMEM)
-    whole = pl.BlockSpec(memory_space=pl.ANY)
+    whole = pl.BlockSpec(memory_space=pltpu.HBM)
     flops = 2 * rows * width * width * tiles * (feeds + joins)
     result = pl.pallas_call(
         functools.partial(kernel, n_lat, n_lon, sides),
         out_shape=jax.ShapeDtypeStruct((rows, tiles * width), jnp.bfloat16),
         in_specs=[smem] * 4 + [whole] * 3,
-        out_specs=whole,
+        out_specs=pl.BlockSpec(memory_space=pltpu.VMEM),
         scratch_shapes=[
             pltpu.VMEM((cells // width, rows, width), jnp.bfloat16),
             pltpu.VMEM((tiles, feeds * width, width), jnp.bfloat16),
             pltpu.VMEM((tiles, joins * width, width), jnp.bfloat16),
-            pltpu.VMEM((rows, tiles * width), jnp.bfloat16),
             pltpu.SemaphoreType.DMA((cells // width,)),
             pltpu.SemaphoreType.DMA((2,)),
-            pltpu.SemaphoreType.DMA((CHUNKS,)),
             pltpu.SemaphoreType.DMA((5 * (2 * spots - 1), CHUNKS)),
             pltpu.SemaphoreType.DMA((5 * spots, CHUNKS)),
         ]
@@ -273,7 +290,7 @@
             for _ in range(CHUNKS)
         ],
         compiler_params=pltpu.CompilerParams(
-            collective_id=0, has_side_effects=True, vmem_limit_bytes=32 * 1024 * 1024
+            collective_id=0, has_side_effects=True, vmem_limit_bytes=56 * 1024 * 1024
         ),
         cost_estimate=pl.CostEstimate(
             flops=flops, bytes_accessed=6 * 1024 * 1024, transcendentals=0

time: 38.1 us -> 29.3 us (0.77)
  local copies, waits for them, and re-layouts: 6.99 us -> 2.26 us
  Pallas kernels: 30.1 us -> 26.1 us
    unnamed x13 -> x1, local copies, waits for them, and re-layouts: 6.99 us -> 2.26 us
    pallas_call x1, Pallas kernels: 30.1 us -> 26.1 us  [body(): pl.pallas_call(functools.partial(kernel, n_lat, n_lon, sides), out_shape=...]
where the time goes in v2:
time: 29.3 us; the launch traced here: 29.1 us
  Pallas kernels  26.1 us (89%)
  local copies, waits for them, and re-layouts  2.26 us (8%)
  between operations  0.66 us (2%)
    pallas_call x1, Pallas kernels, body(): pl.pallas_call(functools.partial(kernel, n_lat, n_lon, sides), out_shape=...  26.1 us
    unnamed x1, local copies, waits for them, and re-layouts  2.26 us

profile of v2, /device:TPU:0, one launch (start us, length us, event | category | flops | bytes accessed | tf_op | source)
XLA Modules:
  0.0 29.1 jit_solution(7022132291400741696)
XLA Ops:
  0.7 26.1 %shard_map.73 = bf16[512,1024]{1,0:T(8,128)(2,1)} custom-call(s32[2,8]{1,0:T(2,128)} %bitcast.16, s32[1,2]{1,0:T(1,128)} %bitcast.17, s32[1,1]{1,0:T(1,128)S(6)} %copy.10.count_ref, s32[8,10]{1,0:T(8,128)} %bitcast.15, bf16[512,1024]{1,0:T(8,128)(2,1)} %bitcast.13, bf16[8,256,128]{2,1,0:T(8,128)(2,1)} %bitcast.14, bf16[8,1280,128]{2,1,0:T(8,128)(2,1)} %bitcast.12), custom_call_target="tpu_custom_call" | custom-call | flops 1610612736 | bytes 6291456 | tf_op jit(solution)/shard_map/pallas_call | solution.py:274
  26.8 2.3 %copy.11 = bf16[8,64,1,1,1024]{4,1,3,2,0:T(8,128)(2,1)} copy(bf16[8,64,1,1,1024]{4,1,3,2,0:T(8,128)(2,1)} %bitcast.11) | data formatting | bytes 2097152

commit v3 on v2

--- a/solution.py
+++ b/solution.py
@@ -16,17 +16,22 @@
     n_lat,
     n_lon,
     sides,
+    blocks_hbm,
+    list_hbm,
+    count_hbm,
+    near_hbm,
+    field_hbm,
+    interp_hbm,
+    conv_hbm,
+    out,
     blocks_ref,
     list_ref,
     count_ref,
     near_ref,
-    field_hbm,
-    interp_hbm,
-    conv_hbm,
-    out,
     field,
     interp,
     conv,
+    index_sem,
     field_sem,
     weight_sem,
     send_sem,
@@ -43,7 +48,17 @@
     spots = 1 + len(sides)
     lat, lon = lax.axis_index("lat"), lax.axis_index("lon")
 
-    loads = [pltpu.make_async_copy(interp_hbm, interp, weight_sem.at[0])]
+    indices = (
+        (blocks_hbm, blocks_ref),
+        (list_hbm, list_ref),
+        (count_hbm, count_ref),
+        (near_hbm, near_ref),
+    )
+    loads = [
+        pltpu.make_async_copy(source, target, index_sem.at[i])
+        for i, (source, target) in enumerate(indices)
+    ]
+    loads.append(pltpu.make_async_copy(interp_hbm, interp, weight_sem.at[0]))
     for k in range(field.shape[0]):
         columns = pl.ds(k * width, width)
         loads.append(
@@ -52,7 +67,6 @@
     conv_load = pltpu.make_async_copy(conv_hbm, conv, weight_sem.at[1])
     for load in loads:
         load.start()
-    conv_load.start()
 
     def inside(band):
         return jnp.logical_and(band >= 0, band < n_lat)
@@ -132,6 +146,7 @@
     near_order, far_order = order[:2], order[2:]
     for load in loads:
         load.wait()
+    conv_load.start()
     for c in range(chunks):
         for h in range(slots):
             value = interpolated(c, list_ref[0, h])
@@ -268,18 +283,22 @@
     cells = model_field.shape[-1]
     sides = (1,) if n_lon == 2 else (1, -1)
     spots = 1 + len(sides)
-    smem = pl.BlockSpec(memory_space=pltpu.SMEM)
     whole = pl.BlockSpec(memory_space=pltpu.HBM)
     flops = 2 * rows * width * width * tiles * (feeds + joins)
     result = pl.pallas_call(
         functools.partial(kernel, n_lat, n_lon, sides),
         out_shape=jax.ShapeDtypeStruct((rows, tiles * width), jnp.bfloat16),
-        in_specs=[smem] * 4 + [whole] * 3,
+        in_specs=[whole] * 7,
         out_specs=pl.BlockSpec(memory_space=pltpu.VMEM),
         scratch_shapes=[
+            pltpu.SMEM((feeds, tiles), jnp.int32),
+            pltpu.SMEM((1, slots), jnp.int32),
+            pltpu.SMEM((1, 1), jnp.int32),
+            pltpu.SMEM((tiles, joins), jnp.int32),
             pltpu.VMEM((cells // width, rows, width), jnp.bfloat16),
             pltpu.VMEM((tiles, feeds * width, width), jnp.bfloat16),
             pltpu.VMEM((tiles, joins * width, width), jnp.bfloat16),
+            pltpu.SemaphoreType.DMA((4,)),
             pltpu.SemaphoreType.DMA((cells // width,)),
             pltpu.SemaphoreType.DMA((2,)),
             pltpu.SemaphoreType.DMA((5 * (2 * spots - 1), CHUNKS)),

time: 29.3 us -> 28.5 us (0.973)
  Pallas kernels: 26.1 us -> 25.4 us
    pallas_call x1, Pallas kernels: 26.1 us -> 25.4 us  [body(): pl.pallas_call(functools.partial(kernel, n_lat, n_lon, sides), out_shape=...]
where the time goes in v3:
time: 28.5 us; the launch traced here: 28.4 us
  Pallas kernels  25.4 us (89%)
  local copies, waits for them, and re-layouts  2.26 us (8%)
  between operations  0.66 us (2%)
    pallas_call x1, Pallas kernels, body(): pl.pallas_call(functools.partial(kernel, n_lat, n_lon, sides), out_shape=...  25.4 us
    unnamed x1, local copies, waits for them, and re-layouts  2.26 us

profile of v3, /device:TPU:0, one launch (start us, length us, event | category | flops | bytes accessed | tf_op | source)
XLA Modules:
  0.0 28.4 jit_solution(2507795452468344312)
XLA Ops:
  0.7 25.4 %shard_map.73 = bf16[512,1024]{1,0:T(8,128)(2,1)} custom-call(s32[2,8]{1,0:T(2,128)} %bitcast.16, s32[1,2]{1,0:T(1,128)} %bitcast.17, s32[1,1]{1,0:T(1,128)S(6)} %copy.10.count_hbm, s32[8,10]{1,0:T(8,128)} %bitcast.15, bf16[512,1024]{1,0:T(8,128)(2,1)} %bitcast.13, bf16[8,256,128]{2,1,0:T(8,128)(2,1)} %bitcast.14, bf16[8,1280,128]{2,1,0:T(8,128)(2,1)} %bitcast.12), custom_call_target="tpu_custom_call" | custom-call | flops 1610612736 | bytes 6291456 | tf_op jit(solution)/shard_map/pallas_call | solution.py:288
  26.1 2.3 %copy.11 = bf16[8,64,1,1,1024]{4,1,3,2,0:T(8,128)(2,1)} copy(bf16[8,64,1,1,1024]{4,1,3,2,0:T(8,128)(2,1)} %bitcast.11) | data formatting | bytes 2097152

commit v4 on v3

--- a/solution.py
+++ b/solution.py
@@ -155,13 +155,14 @@
         if c == 0:
             peers = len(sides) + sum(inside(lat + a).astype(jnp.int32) for a in (1, -1))
             pl.semaphore_wait(barrier, peers)
+        for ai in near_order:
+
+            @pl.when(inside(lat + STEPS[ai]))
+            def _():
+                along_lat(c, ai).start()
+
         for p in range(1, spots):
             along_lon(c, p).start()
-        for ai in near_order:
-
-            @pl.when(inside(lat + STEPS[ai]))
-            def _():
-                along_lat(c, ai).start()
 
     def place(k, n):
         e = near_ref[k, n]

time: 28.5 us -> 28.6 us (level)
  no operation moved by 1% of the time
where the time goes in v4:
time: 28.6 us; the launch traced here: 28.4 us
  Pallas kernels  25.5 us (89%)
  local copies, waits for them, and re-layouts  2.26 us (8%)
  between operations  0.66 us (2%)
    pallas_call x1, Pallas kernels, body(): pl.pallas_call(functools.partial(kernel, n_lat, n_lon, sides), out_shape=...  25.5 us
    unnamed x1, local copies, waits for them, and re-layouts  2.26 us

profile of v4, /device:TPU:0, one launch (start us, length us, event | category | flops | bytes accessed | tf_op | source)
XLA Modules:
  0.0 28.4 jit_solution(15473919003780558244)
XLA Ops:
  0.7 25.5 %shard_map.73 = bf16[512,1024]{1,0:T(8,128)(2,1)} custom-call(s32[2,8]{1,0:T(2,128)} %bitcast.16, s32[1,2]{1,0:T(1,128)} %bitcast.17, s32[1,1]{1,0:T(1,128)S(6)} %copy.10.count_hbm, s32[8,10]{1,0:T(8,128)} %bitcast.15, bf16[512,1024]{1,0:T(8,128)(2,1)} %bitcast.13, bf16[8,256,128]{2,1,0:T(8,128)(2,1)} %bitcast.14, bf16[8,1280,128]{2,1,0:T(8,128)(2,1)} %bitcast.12), custom_call_target="tpu_custom_call" | custom-call | flops 1610612736 | bytes 6291456 | tf_op jit(solution)/shard_map/pallas_call | solution.py:289
  26.1 2.3 %copy.11 = bf16[8,64,1,1,1024]{4,1,3,2,0:T(8,128)(2,1)} copy(bf16[8,64,1,1,1024]{4,1,3,2,0:T(8,128)(2,1)} %bitcast.11) | data formatting | bytes 2097152
